TPU v7x, 256 devices: a whole 4x4x8 slice. The times are simulated.
256 devices in a mesh: tok: 64 (over x, z, core), feat: 4 (over y).
Axes of the slice: x: 4, y: 4, z: 8, core: 2. Of those that a mesh axis runs over, the one named last changes fastest.
Arguments:
- earlier: bfloat16 [65536, 6144], P('tok', 'feat'), may hold values from -6 to 6
- window_x: bfloat16 [65536, 2048], P(('tok', 'feat')), may hold values from -6 to 6
- off_block: bfloat16 [2048, 6144], P('tok', 'feat'), may hold values from -0.078125 to 0.078125
- diag_block: bfloat16 [2048, 2048], P(('tok', 'feat')), as said below
Outputs:
- whitened: float32 [65536, 2048], P(('tok', 'feat'))
Inputs may be any that keep to these rules, and one draw needn't show every extreme that they name: diag_block is lower triangular with diagonal entries between 1 and 3.
All inputs are finite; a program needn't handle non-finite values.
Results may differ from a plain program's by a relative error of at most 0.0003.
Values may be sent and summed in bfloat16 or wider, within the bound.
A program may use at most 128 MiB of HBM per device.

v0:
```python
import jax
import jax.numpy as jnp
from jax import lax
from jax.sharding import PartitionSpec as P


def solve_right(lower, values):
    return lax.linalg.triangular_solve(lower, values, left_side=False, lower=True, transpose_a=True)


def solve_panels(remainder, lower):
    width = lower.shape[0] // 2
    first = solve_right(lower[:width, :width], remainder[:, :width])
    rest = remainder[:, width:] - jnp.dot(
        first,
        lower[width:, :width].T,
        precision=lax.Precision.HIGHEST,
        preferred_element_type=jnp.float32,
    )
    second = solve_right(lower[width:, width:], rest)
    return jnp.concatenate([first, second], axis=1)


def local(earlier, window_x, off_block, diag_block):
    partial_terms = lax.dot_general(
        earlier,
        lax.all_gather(off_block, "tok", axis=0, tiled=True),
        (((1,), (1,)), ((), ())),
        preferred_element_type=jnp.float32,
    )
    shares = lax.psum_scatter(partial_terms, "feat", scatter_dimension=0, tiled=True)
    remainder = window_x.astype(jnp.float32) - shares
    lower = lax.all_gather(diag_block, ("tok", "feat"), axis=0, tiled=True)
    return solve_panels(remainder, lower.astype(jnp.float32))


def solution(mesh):
    return jax.shard_map(
        local,
        mesh=mesh,
        in_specs=(
            P("tok", "feat"),
            P(("tok", "feat"), None),
            P("tok", "feat"),
            P(("tok", "feat"), None),
        ),
        out_specs=P(("tok", "feat"), None),
        check_vma=False,
    )
```

profile of v0, /device:TPU:1, one launch (start us, length us, event | category | flops | bytes accessed | tf_op | source)
XLA Modules:
  0.0 491.4 jit_solution(11038202658564648463)
XLA Ops:
  6.5 0.7 all-gather.5.cloned.1.call-update
  7.3 0.7 all-gather.3.cloned.1.call-update
  8.1 87.4 %all-gather.5.cloned.1.call-done = bf16[2048,1536]{1,0:T(8,128)(2,1)} async-done(((bf16[32,1536]{1,0:T(8,128)(2,1)}), bf16[2048,1536]{1,0:T(8,128)(2,1)}) %all-gather.5.cloned.1.call-update) | async-done | bytes 6291472 | tf_op jit(solution)/shard_map/all_gather | solution.py:27
  95.4 10.9 %fusion.73 = f32[1024,2048]{1,0:T(8,128)} fusion(bf16[1024,1536]{1,0:T(8,128)(2,1)S(1)} %copy-done, bf16[2048,1536]{1,0:T(8,128)(2,1)} %all-gather.5.cloned.1.call-done), kind=kOutput, calls=%fused_computation.163 | convolution fusion | flops 6442450944 | bytes 17825792 | tf_op jit(solution)/shard_map/dot_general | solution.py:25
  106.4 107.5 %all-gather.3.cloned.1.call-done = bf16[2048,2048]{1,0:T(8,128)(2,1)} async-done(((bf16[8,2048]{1,0:T(8,128)(2,1)}), bf16[2048,2048]{1,0:T(8,128)(2,1)}) %all-gather.3.cloned.1.call-update) | async-done | bytes 8388624 | tf_op jit(solution)/shard_map/all_gather | solution.py:33
  213.9 11.8 %convert_element_type.6 = f32[2048,2048]{1,0:T(8,128)} convert(bf16[2048,2048]{1,0:T(8,128)(2,1)} %all-gather.3.cloned.1.call-done) | non-fusion elementwise | flops 4194304 | bytes 25165824 | tf_op jit(solution)/shard_map/convert_element_type | solution.py:34
  225.7 8.1 %slice_select_fusion = (f32[1024,1024]{1,0:T(8,128)}, f32[1024,1024]{1,0:T(8,128)}) fusion(f32[2048,2048]{1,0:T(8,128)} %convert_element_type.6), kind=kLoop, calls=%fused_computation.4 | loop fusion | flops 3145728 | bytes 16777216 | tf_op jit(solution)/shard_map/triangular_solve/select.1 | solution.py:8
  233.9 23.9 %while.4 = (s32[]{:T(128)}, f32[1024,1024]{1,0:T(8,128)}, s32[8,2]{0,1:T(2,128)S(1)}, f32[8,128,128]{2,1,0:T(8,128)S(1)}, s32[]{:T(128)}) while((s32[]{:T(128)}, f32[1024,1024]{1,0:T(8,128)}, s32[8,2]{0,1:T(2,128)S(1)}, f32[8,128,128]{2,1,0:T(8,128)S(1)}, s32[]{:T(128)}) %tuple.80), condition=%wide.while_cond, body=%wide.while_body.sunk | while | flops 2 | bytes 131181 | solution.py:8
  234.0 0.6 fusion.101
  234.6 2.3 bitcast_dynamic-update-slice_fusion.4
  236.9 0.6 fusion.101
  237.5 2.3 bitcast_dynamic-update-slice_fusion.4
  239.9 0.6 fusion.101
  240.5 2.3 bitcast_dynamic-update-slice_fusion.4
  243.5 2.3 bitcast_dynamic-update-slice_fusion.4
  246.5 2.3 bitcast_dynamic-update-slice_fusion.4
  249.5 2.3 bitcast_dynamic-update-slice_fusion.4
  252.5 2.3 bitcast_dynamic-update-slice_fusion.4
  255.5 2.2 bitcast_dynamic-update-slice_fusion.4
  257.8 79.2 %custom-call.4 = f32[8,128,128]{1,2,0:T(8,128)} custom-call(f32[8,128,128]{2,1,0:T(8,128)S(1)} %get-tuple-element.20), custom_call_target="InvertDiagBlocksLowerTriangular" | custom-call | tf_op jit(solution)/shard_map/triangular_solve/custom-call.1 | solution.py:8
  337.1 23.9 %while.5 = (s32[]{:T(128)}, f32[1024,1024]{1,0:T(8,128)}, s32[8,2]{0,1:T(2,128)S(1)}, f32[8,128,128]{2,1,0:T(8,128)S(1)}, s32[]{:T(128)}) while((s32[]{:T(128)}, f32[1024,1024]{1,0:T(8,128)}, s32[8,2]{0,1:T(2,128)S(1)}, f32[8,128,128]{2,1,0:T(8,128)S(1)}, s32[]{:T(128)}) %tuple.92), condition=%wide.while_cond.clone, body=%wide.while_body.clone.sunk | while | flops 2 | bytes 131181 | solution.py:8
  337.7 2.3 bitcast_dynamic-update-slice_fusion.5
  340.7 2.3 bitcast_dynamic-update-slice_fusion.5
  343.7 2.3 bitcast_dynamic-update-slice_fusion.5
  346.7 2.3 bitcast_dynamic-update-slice_fusion.5
  349.7 2.3 bitcast_dynamic-update-slice_fusion.5
  352.7 2.3 bitcast_dynamic-update-slice_fusion.5
  355.7 2.3 bitcast_dynamic-update-slice_fusion.5
  358.7 2.2 bitcast_dynamic-update-slice_fusion.5
  360.9 79.2 %custom-call.5 = f32[8,128,128]{1,2,0:T(8,128)} custom-call(f32[8,128,128]{2,1,0:T(8,128)S(1)} %get-tuple-element.21), custom_call_target="InvertDiagBlocksLowerTriangular" | custom-call | tf_op jit(solution)/shard_map/triangular_solve/custom-call.1 | solution.py:8
  440.2 2.0 convert_subtract_fusion
  442.5 1.2 convolution_subtract_fusion.11
  444.1 1.5 convolution_subtract_fusion.7
  445.9 1.8 convolution_subtract_fusion.6
  448.0 2.0 convolution_subtract_fusion.5
  450.3 2.2 convolution_subtract_fusion.4
  452.9 2.4 convolution_subtract_fusion.10
  455.7 2.7 convolution_subtract_fusion.13
  458.6 5.4 %fusion.2 = f32[256,1024]{1,0:T(8,128)S(1)} fusion(f32[256,1024]{0,1:T(8,128)S(1)} %convolution_dynamic-update-slice_fusion.1, bf16[2048,2048]{1,0:T(8,128)(2,1)} %all-gather.3.cloned.1.call-done, f32[256,2048]{1,0:T(8,128)S(1)} %convert_subtract_fusion), kind=kOutput, calls=%fused_computation.11 | convolution fusion | flops 3221487616 | bytes 5242880 | tf_op jit(solution)/shard_map/dot_general | solution.py:14
  464.4 1.2 convolution_subtract_fusion.9
  466.0 1.5 convolution_subtract_fusion.3
  467.8 1.8 convolution_subtract_fusion.2
  469.9 2.0 convolution_subtract_fusion.1
  472.2 2.2 convolution_subtract_fusion
  474.7 2.4 convolution_subtract_fusion.8
  477.5 2.7 convolution_subtract_fusion.12
  480.5 1.5 pad_maximum_fusion
  482.0 2.9 copy.5
  (64 shorter events, 14.3 us)
Async XLA Ops:
  6.5 88.9 %copy-start = (bf16[1024,1536]{1,0:T(8,128)(2,1)S(1)}, bf16[1024,1536]{1,0:T(8,128)(2,1)}, u32[]{:S(2)}) copy-start(bf16[1024,1536]{1,0:T(8,128)(2,1)} %param.6) | copy-start | bytes 9437188
  6.5 88.9 %all-gather.5.cloned.1.call-start = ((), (), s32[]{:S(2)}) async-start(), calls=%async_computation.2 | async-start | bytes 6389760 | tf_op jit(solution)/shard_map/all_gather | solution.py:27
  7.3 206.6 %all-gather.3.cloned.1.call-start = ((), (), s32[]{:S(2)}) async-start(), calls=%async_computation.1 | async-start | bytes 8421376 | tf_op jit(solution)/shard_map/all_gather | solution.py:33
  8.0 432.2 %reduce-scatter.2.cloned.1.call-start = ((), (), s32[]{:S(2)}) async-start(), calls=%async_computation.3 | async-start | bytes 10485760 | tf_op jit(solution)/shard_map/reduce_scatter | solution.py:31
  225.7 214.5 %copy-start.2 = (bf16[256,2048]{1,0:T(8,128)(2,1)S(1)}, bf16[256,2048]{1,0:T(8,128)(2,1)}, u32[]{:S(2)}) copy-start(bf16[256,2048]{1,0:T(8,128)(2,1)} %param.7) | copy-start | bytes 3145732
  440.2 2.0 copy-start.4
  455.3 8.7 %copy-start.3 = (f32[8,128,128]{1,2,0:T(8,128)S(1)}, f32[8,128,128]{1,2,0:T(8,128)}, u32[]{:S(2)}) copy-start(f32[8,128,128]{1,2,0:T(8,128)} %custom-call.5) | copy-start | bytes 1572868
  480.1 4.7 copy-start.1
Sparse Core Ops, SparseCore 0:
  10.1 85.2 all-gather.4
  99.0 114.8 all-gather.2
  216.5 79.4 reduce-scatter.1
where the time goes:
time: 493 us; the launch traced here: 491 us
  waiting for transfers between devices  196 us (40%)
  other arithmetic  182 us (37%)
  local copies, waits for them, and re-layouts  50.4 us (10%)
  matrix products  48.9 us (10%)
  between operations  13.4 us (3%)
    another operation x4, other arithmetic, solve_right(): lax.linalg.triangular_solve(lower, values, left_side=False, lower=True, t...  167 us
    all_gather x1, waiting for transfers between devices, local(): lower = lax.all_gather(diag_block, ('tok', 'feat'), axis=0, tiled=True)  108 us
    all_gather x1, waiting for transfers between devices, local(): lax.all_gather(off_block, 'tok', axis=0, tiled=True)  87.4 us
    another operation x50, local copies, waits for them, and re-layouts, solve_right(): lax.linalg.triangular_solve(lower, values, left_side=False, lower=True, t...  47.5 us
    another operation x30, matrix products, solve_right(): lax.linalg.triangular_solve(lower, values, left_side=False, lower=True, t...  32.6 us
    convert_element_type x1, other arithmetic, local(): return solve_panels(remainder, lower.astype(jnp.float32))  11.8 us
    dot_general x1, matrix products, local(): lax.dot_general(earlier, lax.all_gather(off_block, 'tok', axis=0, tiled=T...  10.9 us
  transfers between devices with their start and end apart: 3, of which 2 were waited for; matrix products, arithmetic and copies ran while one was open for 48% of the time, Pallas kernels for 0%

commit v1 on v0

v1 whole, which is shorter than its diff:
```python
import jax
import jax.numpy as jnp
from jax import lax
from jax.experimental import pallas as pl
from jax.experimental.pallas import tpu as pltpu
from jax.sharding import PartitionSpec as P

f32, bf16 = jnp.float32, jnp.bfloat16
NX, NY, NZ = 4, 4, 8
WIN, COLS, ROWS, TOK = 2048, 1536, 32, 256
CHUNKS, CW = 16, 128
LAG = 3
FLOOR = 2.0**-10


def split(v):
    high = v.astype(bf16)
    return high, (v - high.astype(f32)).astype(bf16)


def dot(a, b):
    return lax.dot_general(a, b, (((1,), (0,)), ((), ())), preferred_element_type=f32)


def dot_t(a, b):
    return lax.dot_general(a, b, (((1,), (1,)), ((), ())), preferred_element_type=f32)


def dot3(a, b):
    ah, al = split(a)
    bh, bl = split(b)
    return dot(ah, bh) + (dot(ah, bl) + dot(al, bh))


def encode(v):
    m = jnp.abs(v) + FLOOR
    m2 = m * m
    m4 = m2 * m2
    m12 = m4 * m4 * m4
    return jnp.where(v < 0, -m12, m12).astype(bf16)


def decode(code):
    c = code.astype(f32)
    m = jnp.exp(jnp.log(jnp.abs(c)) * (1.0 / 12.0)) - FLOOR
    return jnp.where(c < 0, -m, m)


def inverse(block):
    n = block.shape[0]
    r = lax.broadcasted_iota(jnp.int32, (n, n), 0)
    c = lax.broadcasted_iota(jnp.int32, (n, n), 1)
    differ = r ^ c
    x = jnp.where(differ == 0, 1.0 / jnp.where(differ == 0, block, 1.0), 0.0)
    s = 1
    while s < n:
        below = jnp.where((differ >= s) & (differ < 2 * s), block, 0.0).astype(bf16)
        xh, xl = split(x)
        th, tl = split(dot(xh, below) + dot(xl, below))
        x = x - (dot(th, xh) + (dot(th, xl) + dot(tl, xh)))
        s *= 2
    return x


def kept(xb):
    return 512 * xb + 256


def kernel(e, xw, w, dg, out, wb, db, lb, hs, si, sd, hr, gi, gd, pb, pk, rem, ih, il, acc,
           wz_s, wz_r, wx_s, wx_r, wf_s, ws_s, ws_r, dy_s, dy_r, dx_s, dx_r, dz_s, dz_r, ds_s, ds_r,
           ly_s, ly_r, lx_s, lx_r, lz_s, lz_r, ls_s, ls_r, rs_s, rs_r, in_s, in_r):
    t, y = lax.axis_index("tok"), lax.axis_index("feat")
    x, z, c = lax.div(t, 16), lax.rem(lax.div(t, 2), 8), lax.rem(t, 2)

    def at(dx=0, dy=0, dz=0, dc=0):
        xx, yy = lax.rem(x + dx + NX, NX), lax.rem(y + dy + NY, NY)
        zz, cc = lax.rem(z + dz + NZ, NZ), lax.rem(c + dc, 2)
        return (xx * 16 + zz * 2 + cc, yy)

    def copy(src, ss, rs, device, dst=None):
        return pltpu.make_async_remote_copy(
            src_ref=src, dst_ref=src if dst is None else dst, send_sem=ss, recv_sem=rs,
            device_id=device, device_id_type=pl.DeviceIdType.MESH)

    east, west, up, down, twin = at(dx=1), at(dx=-1), at(dz=1), at(dz=-1), at(dc=1)
    sides = [at(dx=d) for d in (1, 2, 3)]
    others = [at(dy=d) for d in (1, 2, 3)]

    wb[x, z, c] = w[...]
    lb[x, z, c, y] = dg[...]
    db[x, z, c, y] = dg[:, pl.ds(pl.multiple_of((2 * x + lax.div(z, 4)) * 256, 256), 256)]

    barrier = pltpu.get_barrier_semaphore()
    partners = [up, down, twin, *sides, *others]
    for p in partners:
        pl.semaphore_signal(barrier, inc=1, device_id=p, device_id_type=pl.DeviceIdType.MESH)
    pl.semaphore_wait(barrier, len(partners))

    sg = 2 * lax.rem(z, 2) - 1

    def pair_of(k):
        off = jnp.where(k == 0, 0, jnp.where(k == 1, sg, jnp.where(k == 2, -sg, 2)))
        return lax.rem(lax.div(z, 2) + off + 4, 4)

    def chunk_of(s):
        near = jnp.logical_and(s >= 4, s < 12)
        k = jnp.where(s < 4, s, jnp.where(near, lax.div(s - 4, 2), s - 12))
        side = lax.rem(s, 2)
        xs = jnp.where(s < 4, x, jnp.where(near, x + 3 + 2 * side, x + 2))
        return lax.rem(xs, NX), pair_of(k)

    def rows_of(xs, pair, core):
        return wb.at[xs, pl.ds(2 * pair, 2), core]

    def w_ring(k, zsrc, way):
        return copy(wb.at[x, zsrc, c], wz_s.at[way, k], wz_r.at[zsrc], up if way == 0 else down)

    def w_side(s, way):
        return copy(rows_of(x, pair_of(s), c), wx_s.at[way, s], wx_r.at[way, s], east if way == 0 else west)

    def w_far(k, side, xs):
        return copy(rows_of(xs, pair_of(k), c), wf_s.at[k], wx_r.at[2, k], at(dx=1 - 2 * side))

    def w_twin(s, core):
        xs, pair = chunk_of(s)
        return copy(rows_of(xs, pair, core), ws_s.at[s], ws_r.at[s], twin)

    def w_step(s):
        @pl.when(s < 4)
        def _():
            k = s + 1
            zm, zp = lax.rem(z - k + NZ, NZ), lax.rem(z + k, NZ)
            w_ring(0, zm, 0).wait_recv()

            @pl.when(k < 4)
            def _():
                w_ring(k, zm, 0).start()
                w_ring(0, zp, 1).wait_recv()

            @pl.when(k < 3)
            def _():
                w_ring(k, zp, 1).start()

            w_twin(s, c).start()
            w_side(s, 0).start()
            w_side(s, 1).start()

        @pl.when(jnp.logical_and(s >= 4, s < 12))
        def _():
            k, side = lax.div(s - 4, 2), lax.rem(s, 2)
            xs = lax.rem(x + 3 + 2 * side, NX)
            pair = pair_of(k)
            copy(rows_of(xs, pair, c), wx_s.at[0, 0], wx_r.at[side, k], twin).wait_recv()
            w_twin(s, c).start()

            @pl.when(lax.rem(k, 2) == side)
            def _():
                w_far(k, side, xs).start()

        @pl.when(jnp.logical_and(s >= 12, s < CHUNKS))
        def _():
            k = s - 12
            copy(rows_of(lax.rem(x + 2, NX), pair_of(k), c), wx_s.at[0, 0], wx_r.at[2, k], twin).wait_recv()
            w_twin(s, c).start()

    def d_y(d, yy):
        return copy(db.at[x, z, c, yy], dy_s.at[d], dy_r.at[d], others[d])

    def l_y(d, yy):
        return copy(lb.at[x, z, c, yy], ly_s.at[d], ly_r.at[d], others[d])

    def d_x(d, xx):
        return copy(db.at[xx, z, c], dx_s.at[d], dx_r.at[d], sides[d])

    def l_x(d, xx):
        return copy(lb.at[xx, z, c], lx_s.at[d], lx_r.at[d], sides[d])

    def d_ring(k, zsrc, way):
        return copy(db.at[:, zsrc, c], dz_s.at[way, k], dz_r.at[zsrc], up if way == 0 else down)

    def d_twin(zsrc, core):
        return copy(db.at[:, zsrc, core], ds_s.at[zsrc], ds_r.at[zsrc], twin)

    def l_rows(xb, zsrc, core):
        return lb.at[xb, zsrc, core, :, :, pl.ds(0, kept(xb))]

    def l_ring(k, xb, zsrc, way):
        return copy(l_rows(xb, zsrc, c), lz_s.at[way, k, xb], lz_r.at[zsrc, xb], up if way == 0 else down)

    def l_twin(xb, zsrc, core):
        return copy(l_rows(xb, zsrc, core), ls_s.at[zsrc, xb], ls_r.at[zsrc, xb], twin)

    UPPER, LOWER = (0, 3), (1, 2)

    def l_step(k):
        zm, zp = lax.rem(z - k + NZ, NZ), lax.rem(z + k, NZ)
        for xb in range(NX):
            l_ring(0, xb, zm, 0).wait_recv()
            if k < 3 or (k == 3 and xb in UPPER):
                l_ring(k, xb, zm, 0).start()
            l_twin(xb, zm, c).start()
            if k < 4:
                l_ring(0, xb, zp, 1).wait_recv()
                if k < 3 or xb in LOWER:
                    l_ring(k, xb, zp, 1).start()
                l_twin(xb, zp, c).start()

    def factor_step(s):
        @pl.when(s == 0)
        def _():
            for d in range(3):
                d_y(d, lax.rem(y + 3 - d, NY)).wait_recv()
            for d in range(3):
                d_x(d, x).start()
            for d in range(3):
                l_y(d, lax.rem(y + 3 - d, NY)).wait_recv()
            for d in range(3):
                l_x(d, x).start()

        @pl.when(s == 1)
        def _():
            for d in range(3):
                d_x(d, lax.rem(x + 3 - d, NX)).wait_recv()
            d_ring(0, z, 0).start()
            d_ring(0, z, 1).start()
            d_twin(z, c).start()
            for d in range(3):
                l_x(d, lax.rem(x + 3 - d, NX)).wait_recv()
            for xb in range(NX):
                l_ring(0, xb, z, 0).start()
                l_ring(0, xb, z, 1).start()
                l_twin(xb, z, c).start()

        @pl.when(jnp.logical_and(s >= 2, s < 6))
        def _():
            k = s - 1
            zm, zp = lax.rem(z - k + NZ, NZ), lax.rem(z + k, NZ)
            d_ring(0, zm, 0).wait_recv()

            @pl.when(k < 4)
            def _():
                d_ring(k, zm, 0).start()
                d_ring(0, zp, 1).wait_recv()
                d_twin(zp, c).start()

            @pl.when(k < 3)
            def _():
                d_ring(k, zp, 1).start()

            d_twin(zm, c).start()

        @pl.when(s == 6)
        def _():
            for zz in range(NZ):
                d_twin(zz, 1 - c).wait_recv()

        for k, when in ((1, 5), (2, 8), (3, 11), (4, 14)):

            @pl.when(s == when)
            def _(k=k):
                l_step(k)

    def inverse_copies(i, core):
        j = 2 * i + core
        return (copy(ih.at[j], in_s.at[0, i], in_r.at[0, i], twin), copy(il.at[j], in_s.at[1, i], in_r.at[1, i], twin))

    def inverse_step(s):
        @pl.when(jnp.logical_and(s >= 8, lax.rem(s, 2) == 0) & (s < 16))
        def _():
            i = lax.div(s - 8, 2)
            j = 2 * i + c
            block = db[i, pl.ds(4 * c, 4)].reshape(256, 256).astype(f32)
            a, d = inverse(block[:128, :128]), inverse(block[128:, 128:])
            below = block[128:, :128].astype(bf16)
            dh, dl = split(d)
            b = -dot3(dot(dh, below) + dot(dl, below), a)
            for rows, cols, v in ((0, 0, a), (1, 1, d), (1, 0, b), (0, 1, jnp.zeros_like(a))):
                vh, vl = split(v)
                ih[j, pl.ds(128 * rows, 128), pl.ds(128 * cols, 128)] = vh
                il[j, pl.ds(128 * rows, 128), pl.ds(128 * cols, 128)] = vl
            for cp in inverse_copies(i, c):
                cp.start()

    def toward(s):
        return lax.rem(y + 1 + 2 * lax.rem(s, 2), NY)

    def share(n, s):
        to = toward(s) if n != 1 else lax.rem(toward(s) + 2, NY)
        src, dst = ((hs, hr), (si, gi), (sd, gd))[n]
        return copy(src.at[s], rs_s.at[n, s], rs_r.at[n, s], (t, to), dst.at[s])

    def multiply(s):
        xs, pair = chunk_of(s)
        w_twin(s, 1 - c).wait_recv()
        rows = wb[xs, pl.ds(2 * pair, 2)].reshape(CW, COLS)
        pb[...] = dot_t(e[...], rows)

        def part(d):
            return pb[pl.ds(pl.multiple_of(d * TOK, TOK), TOK), :]

        nd = toward(s)
        hs[s] = encode(part(lax.rem(y + 2, NY)))
        share(0, s).start()
        si[s] = encode(part(lax.rem(nd + 2, NY)))
        share(1, s).start()
        pk[lax.rem(s, 2)] = part(nd)
        q = 4 * xs + pair
        rem[q] = xw[:, pl.ds(pl.multiple_of(q * CW, CW), CW)].astype(f32) - part(y)

    def pass_on(s):
        share(0, s).wait_recv()
        sd[s] = encode(pk[lax.rem(s, 2)] + decode(hr[s]))
        share(2, s).start()

    def finish(s):
        xs, pair = chunk_of(s)
        q = 4 * xs + pair
        share(1, s).wait_recv()
        share(2, s).wait_recv()
        rem[q] = rem[q] - (decode(gi[s]) + decode(gd[s]))

    w_ring(0, z, 0).start()
    w_ring(0, z, 1).start()
    for d in range(3):
        d_y(d, y).start()
    for d in range(3):
        l_y(d, y).start()
    w_step(jnp.int32(0))

    @pl.loop(0, CHUNKS + LAG)
    def _(s):
        @pl.when(s < CHUNKS)
        def _():
            multiply(s)

        @pl.when(s + 1 < CHUNKS)
        def _():
            w_step(s + 1)

        factor_step(s)

        @pl.when(jnp.logical_and(s >= 1, s <= CHUNKS))
        def _():
            pass_on(s - 1)

        inverse_step(s)

        @pl.when(s >= LAG)
        def _():
            finish(s - LAG)

    for zz in range(NZ):
        for xb in range(NX):
            l_twin(xb, zz, 1 - c).wait_recv()
    for i in range(4):
        for cp in inverse_copies(i, 1 - c):
            cp.wait_recv()

    for j in range(8):
        v = jnp.concatenate([rem[2 * j], rem[2 * j + 1]], axis=1)
        if j:
            v = v - acc[j]
        vh, vl = split(v)
        o = dot_t(vh, ih[j]) + (dot_t(vh, il[j]) + dot_t(vl, ih[j]))
        out[:, 256 * j : 256 * j + 256] = o
        oh, ol = split(o)
        for i in range(j + 1, 8):
            block = lb[i // 2, pl.ds(4 * (i % 2), 4), :, :, :, pl.ds(256 * j, 256)].reshape(256, 256)
            u = dot_t(oh, block) + dot_t(ol, block)
            acc[i] = u if j == 0 else acc[i] + u

    for k in range(4):
        w_ring(k, z, 0).wait_send()
        if k < 3:
            w_ring(k, z, 1).wait_send()
        w_side(k, 0).wait_send()
        w_side(k, 1).wait_send()
        w_far(k, 0, x).wait_send()
    for s in range(CHUNKS):
        w_twin(s, c).wait_send()
        for n in range(3):
            share(n, s).wait_send()
    for d in range(3):
        for cp in (d_y(d, y), l_y(d, y), d_x(d, x), l_x(d, x)):
            cp.wait_send()
    for k in range(4):
        d_ring(k, z, 0).wait_send()
        if k < 3:
            d_ring(k, z, 1).wait_send()
        for xb in range(NX):
            if k < 3 or xb in UPPER:
                l_ring(k, xb, z, 0).wait_send()
            if k < 3 or xb in LOWER:
                l_ring(k, xb, z, 1).wait_send()
    for zz in range(NZ):
        d_twin(zz, c).wait_send()
        for xb in range(NX):
            l_twin(xb, zz, c).wait_send()
    for i in range(4):
        for cp in inverse_copies(i, c):
            cp.wait_send()


def local(earlier, window_x, off_block, diag_block):
    V, D = pltpu.VMEM, pltpu.SemaphoreType.DMA
    msg = V((CHUNKS, TOK, CW), bf16)
    scratch = [
        V((NX, NZ, 2, ROWS, COLS), bf16),
        V((NX, NZ, 2, NY, 8, 256), bf16),
        V((NX, NZ, 2, NY, 8, WIN), bf16),
        msg, msg, msg, msg, msg, msg,
        V((4 * TOK, CW), f32),
        V((2, TOK, CW), f32),
        V((CHUNKS, TOK, CW), f32),
        V((8, 256, 256), bf16),
        V((8, 256, 256), bf16),
        V((8, TOK, 256), f32),
        D((2, 4)), D((8,)), D((2, 4)), D((3, 4)), D((4,)), D((CHUNKS,)), D((CHUNKS,)),
        D((3,)), D((3,)), D((3,)), D((3,)), D((2, 4)), D((8,)), D((8,)), D((8,)),
        D((3,)), D((3,)), D((3,)), D((3,)), D((2, 4, 4)), D((8, 4)), D((8, 4)), D((8, 4)),
        D((3, CHUNKS)), D((3, CHUNKS)), D((2, 4)), D((2, 4)),
    ]
    return pl.pallas_call(
        kernel,
        out_shape=jax.ShapeDtypeStruct((TOK, WIN), f32),
        in_specs=[pl.BlockSpec(memory_space=pltpu.VMEM)] * 4,
        out_specs=pl.BlockSpec(memory_space=pltpu.VMEM),
        scratch_shapes=scratch,
        name="whiten",
        compiler_params=pltpu.CompilerParams(
            collective_id=0, has_side_effects=True, vmem_limit_bytes=56 * 2**20
        ),
    )(earlier, window_x, off_block, diag_block)


def solution(mesh):
    return jax.shard_map(
        local,
        mesh=mesh,
        in_specs=(
            P("tok", "feat"),
            P(("tok", "feat"), None),
            P("tok", "feat"),
            P(("tok", "feat"), None),
        ),
        out_specs=P(("tok", "feat"), None),
        check_vma=False,
    )
```

time: 493 us -> 105 us (0.21)
  waiting for transfers between devices: 196 us -> 0 us
  other arithmetic: 182 us -> 0 us
  Pallas kernels: 0 us -> 102 us
  matrix products: 48.9 us -> 0 us
  local copies, waits for them, and re-layouts: 50.4 us -> 3.14 us
  between operations: 13.4 us -> 0.01 us
    all_gather x2 -> x0, waiting for transfers between devices: 195 us -> none  [the longest x1 108 us: local(): lower = lax.all_gather(diag_block, ('tok', 'feat'), axis=0, tiled=True)]
    another operation x4 -> x0, other arithmetic: 167 us -> none  [solve_right(): lax.linalg.triangular_solve(lower, values, left_side=False, lower=True, t...]
    pallas_call x0 -> x1, Pallas kernels: none -> 102 us  [local(): pl.pallas_call(kernel, out_shape=jax.ShapeDtypeStruct((TOK, WIN), f32), i...]
    another operation x50 -> x0, local copies, waits for them, and re-layouts: 47.5 us -> none  [solve_right(): lax.linalg.triangular_solve(lower, values, left_side=False, lower=True, t...]
    another operation x30 -> x0, matrix products: 32.6 us -> none  [solve_right(): lax.linalg.triangular_solve(lower, values, left_side=False, lower=True, t...]
    dot_general x2 -> x0, matrix products: 16.3 us -> none  [the longest x1 10.9 us: local(): lax.dot_general(earlier, lax.all_gather(off_block, 'tok', axis=0, tiled=T...]
    convert_element_type x1 -> x0, other arithmetic: 11.8 us -> none  [local(): return solve_panels(remainder, lower.astype(jnp.float32))]
  transfers between devices with their start and end apart: 3 -> 0, of which waited for: 2 -> 0; matrix products, arithmetic and copies ran while one was open for 48% -> 0% of each run, Pallas kernels for 0% -> 0%
where the time goes in v1:
time: 105 us
  Pallas kernels  102 us (97%)
  local copies, waits for them, and re-layouts  3.14 us (3%)
    pallas_call x1, Pallas kernels, local(): pl.pallas_call(kernel, out_shape=jax.ShapeDtypeStruct((TOK, WIN), f32), i...  102 us
    unnamed x1, local copies, waits for them, and re-layouts  3.14 us

profile of v1, /device:TPU:1, one launch (start us, length us, event | category | flops | bytes accessed | tf_op | source)
XLA Modules:
  0.0 105.0 jit_solution(8608939354770498539)
XLA Ops:
  0.0 101.8 %whiten.1 = f32[256,2048]{1,0:T(8,128)} custom-call(bf16[1024,1536]{1,0:T(8,128)(2,1)} %e.1, bf16[256,2048]{1,0:T(8,128)(2,1)} %xw.1, bf16[32,1536]{1,0:T(8,128)(2,1)} %w.1, bf16[8,2048]{1,0:T(8,128)(2,1)} %dg.1), custom_call_target="tpu_custom_call" | custom-call | tf_op jit(solution)/shard_map/whiten/pallas_call | solution.py:423
  101.8 3.1 %copy.6 = f32[256,2048]{1,0:T(8,128)} copy(f32[256,2048]{1,0:T(8,128)} %whiten.1) | data formatting | bytes 4194304

commit v2 on v0

v2 whole, which is shorter than its diff:
```python
import jax
import jax.numpy as jnp
from jax import lax
from jax.experimental import pallas as pl
from jax.experimental.pallas import tpu as pltpu
from jax.sharding import PartitionSpec as P

f32, bf16 = jnp.float32, jnp.bfloat16
NX, NY, NZ = 4, 4, 8
WIN, COLS, ROWS, TOK = 2048, 1536, 32, 256
CHUNKS, CW = 16, 128
TICKS = 9
FLOOR = 2.0**-10


def split(v):
    high = v.astype(bf16)
    return high, (v - high.astype(f32)).astype(bf16)


def dot(a, b):
    return lax.dot_general(a, b, (((1,), (0,)), ((), ())), preferred_element_type=f32)


def dot_t(a, b):
    return lax.dot_general(a, b, (((1,), (1,)), ((), ())), preferred_element_type=f32)


def encode(v):
    m = jnp.abs(v) + FLOOR
    m2 = m * m
    m4 = m2 * m2
    m12 = m4 * m4 * m4
    return jnp.where(v < 0, -m12, m12).astype(bf16)


def decode(code):
    c = code.astype(f32)
    m = jnp.exp(jnp.log(jnp.abs(c)) * (1.0 / 12.0)) - FLOOR
    return jnp.where(c < 0, -m, m)


def inverse(block):
    n = block.shape[0]
    r = lax.broadcasted_iota(jnp.int32, (n, n), 0)
    c = lax.broadcasted_iota(jnp.int32, (n, n), 1)
    differ = r ^ c
    x = jnp.where(differ == 0, 1.0 / jnp.where(differ == 0, block, 1.0), 0.0)
    s = 1
    while s < n:
        below = jnp.where((differ >= s) & (differ < 2 * s), block, 0.0).astype(bf16)
        xh, xl = split(x)
        th, tl = split(dot(xh, below) + dot(xl, below))
        x = x - (dot(th, xh) + (dot(th, xl) + dot(tl, xh)))
        s *= 2
    return x


def kept(xb):
    return 512 * xb + 384


def kernel(e_hbm, x_hbm, w, dg, out_hbm, e, xw, ov, wb, gb, iv, vb, lb, hs, si, sd, hr, gi, gd, pb, pk, rem, ih, il, acc,
           in_s, out_s, wz_s, wz_r, wx_s, wx_r, wf_s, ws_s, ws_r, gy_s, gy_r, gg_s, gg_r, vx_s, vx_r, vz_s, vz_r, vt_s, vt_r,
           lx_s, lx_r, ly_s, ly_r, lz_s, lz_r, lt_s, lt_r, rs_s, rs_r):
    t, y = lax.axis_index("tok"), lax.axis_index("feat")
    x, z, c = lax.div(t, 16), lax.rem(lax.div(t, 2), 8), lax.rem(t, 2)
    low = lax.rem(z, 2)

    def at(dx=0, dy=0, dz=0, dc=0):
        xx, yy = lax.rem(x + dx + NX, NX), lax.rem(y + dy + NY, NY)
        zz, cc = lax.rem(z + dz + NZ, NZ), lax.rem(c + dc, 2)
        return (xx * 16 + zz * 2 + cc, yy)

    def copy(src, ss, rs, device, dst=None):
        return pltpu.make_async_remote_copy(
            src_ref=src, dst_ref=src if dst is None else dst, send_sem=ss, recv_sem=rs,
            device_id=device, device_id_type=pl.DeviceIdType.MESH)

    load_e = pltpu.make_async_copy(e_hbm, e, in_s.at[0])
    load_x = pltpu.make_async_copy(x_hbm, xw, in_s.at[1])
    load_e.start()
    load_x.start()

    east, west, up, down, twin = at(dx=1), at(dx=-1), at(dz=1), at(dz=-1), at(dc=1)
    mates = [twin, at(dz=1 - 2 * low), at(dz=1 - 2 * low, dc=1)]
    sides = [at(dx=d) for d in (1, 2, 3)]
    others = [at(dy=d) for d in (1, 2, 3)]

    wb[x, z, c] = w[...]
    lb[x, z, c, y] = dg[...]
    gb[low, c, y] = dg[:, pl.ds(pl.multiple_of(lax.div(t, 4) * 128, 128), 128)]

    barrier = pltpu.get_barrier_semaphore()
    partners = [up, down, twin, mates[2], *sides, *others]
    for p in partners:
        pl.semaphore_signal(barrier, inc=1, device_id=p, device_id_type=pl.DeviceIdType.MESH)
    pl.semaphore_wait(barrier, len(partners))

    sg = 2 * low - 1

    def pair_of(k):
        off = jnp.where(k == 0, 0, jnp.where(k == 1, sg, jnp.where(k == 2, -sg, 2)))
        return lax.rem(lax.div(z, 2) + off + 4, 4)

    def chunk_of(n):
        side, g = lax.rem(n, 2), lax.div(n, 2)
        own = jnp.logical_or(g == 0, g == 3)
        far = g >= 6
        near_k = jnp.where(g < 3, g - 1, g - 2)
        k = jnp.where(own, jnp.where(g == 0, side, 2 + side), jnp.where(far, n - 12, near_k))
        xs = jnp.where(own, x, jnp.where(far, x + 2, x + 3 + 2 * side))
        return lax.rem(xs, NX), pair_of(k)

    def rows_of(xs, pair, core):
        return wb.at[xs, pl.ds(2 * pair, 2), core]

    def w_ring(k, zsrc, way):
        return copy(wb.at[x, zsrc, c], wz_s.at[way, k], wz_r.at[zsrc], up if way == 0 else down)

    def w_side(k, way):
        return copy(rows_of(x, pair_of(k), c), wx_s.at[way, k], wx_r.at[way, k], east if way == 0 else west)

    def w_near(k, side):
        return copy(rows_of(lax.rem(x + 3 + 2 * side, NX), pair_of(k), c), wf_s.at[k], wx_r.at[side, k], twin)

    def w_on(k):
        side = k % 2
        return copy(rows_of(lax.rem(x + 3 + 2 * side, NX), pair_of(k), c), wf_s.at[k], wx_r.at[2, k], (east, west)[side])

    def w_far(k):
        return copy(rows_of(lax.rem(x + 2, NX), pair_of(k), c), wf_s.at[k], wx_r.at[2, k], twin)

    def w_twin(n, core):
        xs, pair = chunk_of(n)
        return copy(rows_of(xs, pair, core), ws_s.at[n], ws_r.at[n], twin)

    def own_step(k):
        zm, zp = lax.rem(z - (k + 1) + NZ, NZ), lax.rem(z + k + 1, NZ)
        w_ring(0, zm, 0).wait_recv()
        if k < 3:
            w_ring(k + 1, zm, 0).start()
            w_ring(0, zp, 1).wait_recv()
        if k < 2:
            w_ring(k + 1, zp, 1).start()
        w_twin(jnp.int32((0, 1, 6, 7)[k]), c).start()
        w_side(k, 0).start()
        w_side(k, 1).start()

    def near_step(k):
        for side in (0, 1):
            w_near(k, side).wait_recv()
            if side == k % 2:
                w_on(k).start()
            w_twin(jnp.int32((2, 4, 8, 10)[k] + side), c).start()

    def far_step(k):
        w_far(k).wait_recv()
        w_twin(jnp.int32(12 + k), c).start()

    def fetch(tick):
        @pl.when(tick == 0)
        def _():
            own_step(1)

        @pl.when(tick == 1)
        def _():
            own_step(2)
            near_step(0)

        @pl.when(tick == 2)
        def _():
            own_step(3)
            near_step(1)

        @pl.when(tick == 3)
        def _():
            near_step(2)

        @pl.when(tick == 5)
        def _():
            near_step(3)

        @pl.when(tick == 6)
        def _():
            far_step(0)
            far_step(1)

        @pl.when(tick == 7)
        def _():
            far_step(2)
            far_step(3)

    def g_y(d, yy):
        return copy(gb.at[low, c, yy], gy_s.at[d], gy_r.at[d], others[d])

    def g_mate(i, zl, core):
        return copy(gb.at[zl, core], gg_s.at[i], gg_r.at[i], mates[i])

    def v_x(d, xx):
        return copy(vb.at[xx, z, c], vx_s.at[d], vx_r.at[d], sides[d])

    def v_ring(k, zsrc, way):
        return copy(vb.at[:, zsrc, c], vz_s.at[way, k], vz_r.at[zsrc], up if way == 0 else down)

    def v_twin(zsrc, core):
        return copy(vb.at[:, zsrc, core], vt_s.at[zsrc], vt_r.at[zsrc], twin)

    def invert():
        g_mate(0, low, 1 - c).wait_recv()
        g_mate(1, 1 - low, c).wait_recv()
        g_mate(2, 1 - low, 1 - c).wait_recv()
        iv[0], iv[1] = split(inverse(gb[...].reshape(128, 128).astype(f32)))
        mine = pl.ds(pl.multiple_of(32 * (2 * low + c), 32), 32)
        vb[x, z, c, 0] = iv[0, mine]
        vb[x, z, c, 1] = iv[1, mine]
        for d in range(3):
            v_x(d, x).start()

    def v_step(k):
        if k == 0:
            for d in range(3):
                v_x(d, lax.rem(x + 3 - d, NX)).wait_recv()
            v_ring(0, z, 0).start()
            v_ring(0, z, 1).start()
            v_twin(z, c).start()
            return
        zm, zp = lax.rem(z - k + NZ, NZ), lax.rem(z + k, NZ)
        v_ring(0, zm, 0).wait_recv()
        if k < 4:
            v_ring(k, zm, 0).start()
            v_ring(0, zp, 1).wait_recv()
            if k < 3:
                v_ring(k, zp, 1).start()
            v_twin(zp, c).start()
        v_twin(zm, c).start()

    def l_x(d, xx):
        return copy(lb.at[xx, z, c, y], lx_s.at[d], lx_r.at[d], sides[d])

    def l_y(d, xb, yy):
        return copy(lb.at[xb, z, c, yy, :, pl.ds(0, kept(xb))], ly_s.at[d, xb], ly_r.at[d, xb], others[d])

    def l_rows(xb, zsrc, core):
        return lb.at[xb, zsrc, core, :, :, pl.ds(0, kept(xb))]

    def l_ring(k, xb, zsrc, way):
        return copy(l_rows(xb, zsrc, c), lz_s.at[way, k, xb], lz_r.at[zsrc, xb], up if way == 0 else down)

    def l_twin(xb, zsrc, core):
        return copy(l_rows(xb, zsrc, core), lt_s.at[zsrc, xb], lt_r.at[zsrc, xb], twin)

    UPPER, LOWER = (0, 3), (1, 2)

    def l_step(k):
        if k == 0:
            for xb in range(NX):
                for d in range(3):
                    l_y(d, xb, lax.rem(y + 3 - d, NY)).wait_recv()
                l_ring(0, xb, z, 0).start()
                l_ring(0, xb, z, 1).start()
                l_twin(xb, z, c).start()
            return
        zm, zp = lax.rem(z - k + NZ, NZ), lax.rem(z + k, NZ)
        for xb in range(NX):
            l_ring(0, xb, zm, 0).wait_recv()
            if k < 3 or (k == 3 and xb in UPPER):
                l_ring(k, xb, zm, 0).start()
            l_twin(xb, zm, c).start()
            if k < 4:
                l_ring(0, xb, zp, 1).wait_recv()
                if k < 3 or xb in LOWER:
                    l_ring(k, xb, zp, 1).start()
                l_twin(xb, zp, c).start()

    def join():
        for zz in range(NZ):
            v_twin(zz, 1 - c).wait_recv()
            for xb in range(NX):
                l_twin(xb, zz, 1 - c).wait_recv()
        for j in range(8):
            xb, first = j // 2, 4 * (j % 2)
            ah, al = (vb[xb, pl.ds(first, 2), :, h].reshape(128, 128) for h in (0, 1))
            dh, dl = (vb[xb, pl.ds(first + 2, 2), :, h].reshape(128, 128) for h in (0, 1))
            below = lb[xb, pl.ds(first + 2, 2), :, :, :, pl.ds(256 * j, 128)].reshape(128, 128)
            th, tl = split(dot(dh, below) + dot(dl, below))
            bh, bl = split(-(dot(th, ah) + (dot(th, al) + dot(tl, ah))))
            zero = jnp.zeros((128, 128), bf16)
            for ref, parts in ((ih, (ah, zero, bh, dh)), (il, (al, zero, bl, dl))):
                ref[j, :128, :128] = parts[0]
                ref[j, :128, 128:] = parts[1]
                ref[j, 128:, :128] = parts[2]
                ref[j, 128:, 128:] = parts[3]

    def factor(tick):
        @pl.when(tick == 0)
        def _():
            invert()

        @pl.when(tick == 1)
        def _():
            l_step(0)

        @pl.when(tick == 3)
        def _():
            v_step(0)

        @pl.when(tick == 4)
        def _():
            v_step(1)
            l_step(1)

        @pl.when(tick == 5)
        def _():
            v_step(2)

        @pl.when(tick == 6)
        def _():
            v_step(3)
            l_step(2)

        @pl.when(tick == 7)
        def _():
            v_step(4)

        @pl.when(tick == 8)
        def _():
            l_step(3)

        @pl.when(tick == 9)
        def _():
            l_step(4)
            join()

    def toward(n):
        return lax.rem(y + 1 + 2 * lax.rem(n, 2), NY)

    def share(kind, n):
        to = toward(n) if kind != 1 else lax.rem(toward(n) + 2, NY)
        src, dst = ((hs, hr), (si, gi), (sd, gd))[kind]
        return copy(src.at[n], rs_s.at[kind, n], rs_r.at[kind, n], (t, to), dst.at[n])

    def rows(n):
        xs, pair = chunk_of(n)
        w_twin(n, 1 - c).wait_recv()
        return wb[xs, pl.ds(2 * pair, 2)].reshape(CW, COLS)

    def hand_out(n, i):
        def part(d):
            return pb[pl.ds(pl.multiple_of(d * TOK, TOK), TOK), pl.ds(CW * i, CW)]

        nd = toward(n)
        hs[n] = encode(part(lax.rem(y + 2, NY)))
        share(0, n).start()
        si[n] = encode(part(lax.rem(nd + 2, NY)))
        share(1, n).start()
        pk[lax.rem(n, 4)] = part(nd)
        xs, pair = chunk_of(n)
        q = 4 * xs + pair
        rem[q] = xw[:, pl.ds(pl.multiple_of(q * CW, CW), CW)].astype(f32) - part(y)

    def pass_on(n):
        share(0, n).wait_recv()
        sd[n] = encode(pk[lax.rem(n, 4)] + decode(hr[n]))
        share(2, n).start()

    def finish(n):
        xs, pair = chunk_of(n)
        q = 4 * xs + pair
        share(1, n).wait_recv()
        share(2, n).wait_recv()
        rem[q] = rem[q] - (decode(gi[n]) + decode(gd[n]))

    def each(tick, do):
        n = jnp.where(tick < 2, tick, 2 * tick - 2)
        do(n)

        @pl.when(tick >= 2)
        def _():
            do(n + 1)

    w_ring(0, z, 0).start()
    w_ring(0, z, 1).start()
    for d in range(3):
        g_y(d, y).start()
    for d in range(3):
        l_x(d, x).start()
    own_step(0)
    for d in range(3):
        g_y(d, lax.rem(y + 3 - d, NY)).wait_recv()
    for i in range(3):
        g_mate(i, low, c).start()
    for d in range(3):
        l_x(d, lax.rem(x + 3 - d, NX)).wait_recv()
    for xb in range(NX):
        for d in range(3):
            l_y(d, xb, y).start()
    load_e.wait()
    load_x.wait()

    @pl.loop(0, TICKS + 2)
    def _(tick):
        @pl.when(tick < 2)
        def _():
            pb[:, pl.ds(0, CW)] = dot_t(e[...], rows(tick))
            hand_out(tick, 0)

        @pl.when(jnp.logical_and(tick >= 2, tick < TICKS))
        def _():
            n = 2 * tick - 2
            pb[...] = dot_t(e[...], jnp.concatenate([rows(n), rows(n + 1)], axis=0))
            hand_out(n, 0)
            hand_out(n + 1, 1)

        fetch(tick)

        @pl.when(jnp.logical_and(tick >= 1, tick <= TICKS))
        def _():
            each(tick - 1, pass_on)

        @pl.when(tick >= 2)
        def _():
            each(tick - 2, finish)

        factor(tick)

    def store(j):
        return pltpu.make_async_copy(ov.at[j], out_hbm.at[:, pl.ds(256 * j, 256)], out_s.at[j])

    for j in range(8):
        v = jnp.concatenate([rem[2 * j], rem[2 * j + 1]], axis=1)
        if j:
            v = v - acc[j]
        vh, vl = split(v)
        o = dot_t(vh, ih[j]) + (dot_t(vh, il[j]) + dot_t(vl, ih[j]))
        ov[j] = o
        store(j).start()
        oh, ol = split(o)
        for i in range(j + 1, 8):
            block = lb[i // 2, pl.ds(4 * (i % 2), 4), :, :, :, pl.ds(256 * j, 256)].reshape(256, 256)
            u = dot_t(oh, block) + dot_t(ol, block)
            acc[i] = u if j == 0 else acc[i] + u

    for k in range(4):
        w_ring(k, z, 0).wait_send()
        if k < 3:
            w_ring(k, z, 1).wait_send()
        w_side(k, 0).wait_send()
        w_side(k, 1).wait_send()
        w_on(k).wait_send()
    for n in range(CHUNKS):
        w_twin(n, c).wait_send()
        for kind in range(3):
            share(kind, n).wait_send()
    for d in range(3):
        for cp in (g_y(d, y), g_mate(d, low, c), v_x(d, x), l_x(d, x)):
            cp.wait_send()
        for xb in range(NX):
            l_y(d, xb, y).wait_send()
    for k in range(4):
        v_ring(k, z, 0).wait_send()
        if k < 3:
            v_ring(k, z, 1).wait_send()
        for xb in range(NX):
            if k < 3 or xb in UPPER:
                l_ring(k, xb, z, 0).wait_send()
            if k < 3 or xb in LOWER:
                l_ring(k, xb, z, 1).wait_send()
    for zz in range(NZ):
        v_twin(zz, c).wait_send()
        for xb in range(NX):
            l_twin(xb, zz, c).wait_send()
    for j in range(8):
        store(j).wait()


def local(earlier, window_x, off_block, diag_block):
    V, D = pltpu.VMEM, pltpu.SemaphoreType.DMA
    msg = V((CHUNKS, TOK, CW), bf16)
    scratch = [
        V((4 * TOK, COLS), bf16),
        V((TOK, WIN), bf16),
        V((8, TOK, 256), f32),
        V((NX, NZ, 2, ROWS, COLS), bf16),
        V((2, 2, NY, 8, 128), bf16),
        V((2, 128, 128), bf16),
        V((NX, NZ, 2, 2, ROWS, 128), bf16),
        V((NX, NZ, 2, NY, 8, WIN), bf16),
        msg, msg, msg, msg, msg, msg,
        V((4 * TOK, 2 * CW), f32),
        V((4, TOK, CW), f32),
        V((CHUNKS, TOK, CW), f32),
        V((8, 256, 256), bf16),
        V((8, 256, 256), bf16),
        V((8, TOK, 256), f32),
        D((2,)), D((8,)),
        D((2, 4)), D((8,)), D((2, 4)), D((3, 4)), D((4,)), D((CHUNKS,)), D((CHUNKS,)),
        D((3,)), D((3,)), D((3,)), D((3,)), D((3,)), D((3,)), D((2, 4)), D((8,)), D((8,)), D((8,)),
        D((3,)), D((3,)), D((3, 4)), D((3, 4)), D((2, 4, 4)), D((8, 4)), D((8, 4)), D((8, 4)),
        D((3, CHUNKS)), D((3, CHUNKS)),
    ]
    return pl.pallas_call(
        kernel,
        out_shape=jax.ShapeDtypeStruct((TOK, WIN), f32),
        in_specs=[pl.BlockSpec(memory_space=pl.ANY)] * 2 + [pl.BlockSpec(memory_space=V)] * 2,
        out_specs=pl.BlockSpec(memory_space=pl.ANY),
        scratch_shapes=scratch,
        name="whiten",
        compiler_params=pltpu.CompilerParams(
            collective_id=0, has_side_effects=True, vmem_limit_bytes=56 * 2**20
        ),
    )(earlier, window_x, off_block, diag_block)


def solution(mesh):
    return jax.shard_map(
        local,
        mesh=mesh,
        in_specs=(
            P("tok", "feat"),
            P(("tok", "feat"), None),
            P("tok", "feat"),
            P(("tok", "feat"), None),
        ),
        out_specs=P(("tok", "feat"), None),
        check_vma=False,
    )
```

time: 493 us -> 77.3 us (0.16)
  waiting for transfers between devices: 196 us -> 0 us
  other arithmetic: 182 us -> 0 us
  Pallas kernels: 0 us -> 74 us
  matrix products: 48.9 us -> 0 us
  local copies, waits for them, and re-layouts: 50.4 us -> 3.14 us
  between operations: 13.4 us -> 0.01 us
    all_gather x2 -> x0, waiting for transfers between devices: 195 us -> none  [the longest x1 108 us: local(): lower = lax.all_gather(diag_block, ('tok', 'feat'), axis=0, tiled=True)]
    another operation x4 -> x0, other arithmetic: 167 us -> none  [solve_right(): lax.linalg.triangular_solve(lower, values, left_side=False, lower=True, t...]
    pallas_call x0 -> x1, Pallas kernels: none -> 74 us  [local(): pl.pallas_call(kernel, out_shape=jax.ShapeDtypeStruct((TOK, WIN), f32), i...]
    another operation x50 -> x0, local copies, waits for them, and re-layouts: 47.5 us -> none  [solve_right(): lax.linalg.triangular_solve(lower, values, left_side=False, lower=True, t...]
    another operation x30 -> x0, matrix products: 32.6 us -> none  [solve_right(): lax.linalg.triangular_solve(lower, values, left_side=False, lower=True, t...]
    dot_general x2 -> x0, matrix products: 16.3 us -> none  [the longest x1 10.9 us: local(): lax.dot_general(earlier, lax.all_gather(off_block, 'tok', axis=0, tiled=T...]
    convert_element_type x1 -> x0, other arithmetic: 11.8 us -> none  [local(): return solve_panels(remainder, lower.astype(jnp.float32))]
  transfers between devices with their start and end apart: 3 -> 0, of which waited for: 2 -> 0; matrix products, arithmetic and copies ran while one was open for 48% -> 0% of each run, Pallas kernels for 0% -> 0%
where the time goes in v2:
time: 77.3 us; the launch traced here: 77.2 us
  Pallas kernels  74 us (96%)
  local copies, waits for them, and re-layouts  3.14 us (4%)
    pallas_call x1, Pallas kernels, local(): pl.pallas_call(kernel, out_shape=jax.ShapeDtypeStruct((TOK, WIN), f32), i...  74 us
    unnamed x1, local copies, waits for them, and re-layouts  3.14 us

profile of v2, /device:TPU:1, one launch (start us, length us, event | category | flops | bytes accessed | tf_op | source)
XLA Modules:
  0.0 77.2 jit_solution(2719051616449977096)
XLA Ops:
  0.0 74.0 %whiten.1 = f32[256,2048]{1,0:T(8,128)} custom-call(bf16[1024,1536]{1,0:T(8,128)(2,1)} %e_hbm.1, bf16[256,2048]{1,0:T(8,128)(2,1)} %x_hbm.1, bf16[32,1536]{1,0:T(8,128)(2,1)} %w.1, bf16[8,2048]{1,0:T(8,128)(2,1)} %dg.1), custom_call_target="tpu_custom_call" | custom-call | tf_op jit(solution)/shard_map/whiten/pallas_call | solution.py:502
  74.0 3.1 %copy.6 = f32[256,2048]{1,0:T(8,128)} copy(f32[256,2048]{1,0:T(8,128)} %whiten.1) | data formatting | bytes 4194304

commit v3 on v2

--- a/solution.py
+++ b/solution.py
@@ -56,11 +56,11 @@
     return x
 
 
-def kept(xb):
-    return 512 * xb + 384
-
-
-def kernel(e_hbm, x_hbm, w, dg, out_hbm, e, xw, ov, wb, gb, iv, vb, lb, hs, si, sd, hr, gi, gd, pb, pk, rem, ih, il, acc,
+FIRST = (0, 3, 10, 21)
+PACKED, HALF = 36, 18
+
+
+def kernel(e_hbm, x_hbm, w_hbm, dg_hbm, out_hbm, e, xw, dg, ov, wb, gb, iv, vb, lx, lp, hs, si, sd, hr, gi, gd, pb, pk, rem, ih, il, acc,
            in_s, out_s, wz_s, wz_r, wx_s, wx_r, wf_s, ws_s, ws_r, gy_s, gy_r, gg_s, gg_r, vx_s, vx_r, vz_s, vz_r, vt_s, vt_r,
            lx_s, lx_r, ly_s, ly_r, lz_s, lz_r, lt_s, lt_r, rs_s, rs_r):
     t, y = lax.axis_index("tok"), lax.axis_index("feat")
@@ -77,19 +77,17 @@
             src_ref=src, dst_ref=src if dst is None else dst, send_sem=ss, recv_sem=rs,
             device_id=device, device_id_type=pl.DeviceIdType.MESH)
 
-    load_e = pltpu.make_async_copy(e_hbm, e, in_s.at[0])
-    load_x = pltpu.make_async_copy(x_hbm, xw, in_s.at[1])
-    load_e.start()
-    load_x.start()
+    load_w = pltpu.make_async_copy(w_hbm, wb.at[x, z, c], in_s.at[0])
+    load_dg = pltpu.make_async_copy(dg_hbm, dg, in_s.at[1])
+    load_e = pltpu.make_async_copy(e_hbm, e, in_s.at[2])
+    load_x = pltpu.make_async_copy(x_hbm, xw, in_s.at[3])
+    for load in (load_w, load_dg, load_e, load_x):
+        load.start()
 
     east, west, up, down, twin = at(dx=1), at(dx=-1), at(dz=1), at(dz=-1), at(dc=1)
     mates = [twin, at(dz=1 - 2 * low), at(dz=1 - 2 * low, dc=1)]
     sides = [at(dx=d) for d in (1, 2, 3)]
     others = [at(dy=d) for d in (1, 2, 3)]
-
-    wb[x, z, c] = w[...]
-    lb[x, z, c, y] = dg[...]
-    gb[low, c, y] = dg[:, pl.ds(pl.multiple_of(lax.div(t, 4) * 128, 128), 128)]
 
     barrier = pltpu.get_barrier_semaphore()
     partners = [up, down, twin, mates[2], *sides, *others]
@@ -157,39 +155,6 @@
     def far_step(k):
         w_far(k).wait_recv()
         w_twin(jnp.int32(12 + k), c).start()
-
-    def fetch(tick):
-        @pl.when(tick == 0)
-        def _():
-            own_step(1)
-
-        @pl.when(tick == 1)
-        def _():
-            own_step(2)
-            near_step(0)
-
-        @pl.when(tick == 2)
-        def _():
-            own_step(3)
-            near_step(1)
-
-        @pl.when(tick == 3)
-        def _():
-            near_step(2)
-
-        @pl.when(tick == 5)
-        def _():
-            near_step(3)
-
-        @pl.when(tick == 6)
-        def _():
-            far_step(0)
-            far_step(1)
-
-        @pl.when(tick == 7)
-        def _():
-            far_step(2)
-            far_step(3)
 
     def g_y(d, yy):
         return copy(gb.at[low, c, yy], gy_s.at[d], gy_r.at[d], others[d])
@@ -236,53 +201,57 @@
         v_twin(zm, c).start()
 
     def l_x(d, xx):
-        return copy(lb.at[xx, z, c, y], lx_s.at[d], lx_r.at[d], sides[d])
-
-    def l_y(d, xb, yy):
-        return copy(lb.at[xb, z, c, yy, :, pl.ds(0, kept(xb))], ly_s.at[d, xb], ly_r.at[d, xb], others[d])
-
-    def l_rows(xb, zsrc, core):
-        return lb.at[xb, zsrc, core, :, :, pl.ds(0, kept(xb))]
-
-    def l_ring(k, xb, zsrc, way):
-        return copy(l_rows(xb, zsrc, c), lz_s.at[way, k, xb], lz_r.at[zsrc, xb], up if way == 0 else down)
-
-    def l_twin(xb, zsrc, core):
-        return copy(l_rows(xb, zsrc, core), lt_s.at[zsrc, xb], lt_r.at[zsrc, xb], twin)
-
-    UPPER, LOWER = (0, 3), (1, 2)
+        return copy(lx.at[xx], lx_s.at[d], lx_r.at[d], sides[d])
+
+    def l_pack():
+        for xb in range(NX):
+            for b in range(4 * xb + 3):
+                lp[z, c, FIRST[xb] + b, y] = lx[xb, :, 128 * b : 128 * b + 128]
+
+    def l_y(d, yy):
+        return copy(lp.at[z, c, :, yy], ly_s.at[d], ly_r.at[d], others[d])
+
+    def l_ring(k, zsrc, way):
+        return copy(lp.at[zsrc, c], lz_s.at[way, k], lz_r.at[zsrc, 0], up if way == 0 else down)
+
+    def l_last(zsrc, way):
+        half = lp.at[zsrc, c, pl.ds(HALF * way, HALF)]
+        return copy(half, lz_s.at[way, 3], lz_r.at[zsrc, way], up if way == 0 else down)
+
+    def l_twin(zsrc, core):
+        return copy(lp.at[zsrc, core], lt_s.at[zsrc], lt_r.at[zsrc], twin)
 
     def l_step(k):
         if k == 0:
-            for xb in range(NX):
-                for d in range(3):
-                    l_y(d, xb, lax.rem(y + 3 - d, NY)).wait_recv()
-                l_ring(0, xb, z, 0).start()
-                l_ring(0, xb, z, 1).start()
-                l_twin(xb, z, c).start()
+            for d in range(3):
+                l_y(d, lax.rem(y + 3 - d, NY)).wait_recv()
+            l_ring(0, z, 0).start()
+            l_ring(0, z, 1).start()
+            l_twin(z, c).start()
             return
         zm, zp = lax.rem(z - k + NZ, NZ), lax.rem(z + k, NZ)
-        for xb in range(NX):
-            l_ring(0, xb, zm, 0).wait_recv()
-            if k < 3 or (k == 3 and xb in UPPER):
-                l_ring(k, xb, zm, 0).start()
-            l_twin(xb, zm, c).start()
-            if k < 4:
-                l_ring(0, xb, zp, 1).wait_recv()
-                if k < 3 or xb in LOWER:
-                    l_ring(k, xb, zp, 1).start()
-                l_twin(xb, zp, c).start()
+        if k == 4:
+            l_last(zm, 0).wait_recv()
+            l_last(zm, 1).wait_recv()
+            l_twin(zm, c).start()
+            return
+        for zsrc, way in ((zm, 0), (zp, 1)):
+            l_ring(0, zsrc, way).wait_recv()
+            if k < 3:
+                l_ring(k, zsrc, way).start()
+            else:
+                l_last(zsrc, way).start()
+            l_twin(zsrc, c).start()
 
     def join():
         for zz in range(NZ):
             v_twin(zz, 1 - c).wait_recv()
-            for xb in range(NX):
-                l_twin(xb, zz, 1 - c).wait_recv()
+            l_twin(zz, 1 - c).wait_recv()
         for j in range(8):
             xb, first = j // 2, 4 * (j % 2)
             ah, al = (vb[xb, pl.ds(first, 2), :, h].reshape(128, 128) for h in (0, 1))
             dh, dl = (vb[xb, pl.ds(first + 2, 2), :, h].reshape(128, 128) for h in (0, 1))
-            below = lb[xb, pl.ds(first + 2, 2), :, :, :, pl.ds(256 * j, 128)].reshape(128, 128)
+            below = lp[pl.ds(first + 2, 2), :, FIRST[xb] + 2 * j].reshape(128, 128)
             th, tl = split(dot(dh, below) + dot(dl, below))
             bh, bl = split(-(dot(th, ah) + (dot(th, al) + dot(tl, ah))))
             zero = jnp.zeros((128, 128), bf16)
@@ -292,45 +261,39 @@
                 ref[j, 128:, :128] = parts[2]
                 ref[j, 128:, 128:] = parts[3]
 
-    def factor(tick):
-        @pl.when(tick == 0)
-        def _():
-            invert()
-
-        @pl.when(tick == 1)
-        def _():
-            l_step(0)
-
-        @pl.when(tick == 3)
-        def _():
-            v_step(0)
-
-        @pl.when(tick == 4)
-        def _():
-            v_step(1)
-            l_step(1)
-
-        @pl.when(tick == 5)
-        def _():
-            v_step(2)
-
-        @pl.when(tick == 6)
-        def _():
-            v_step(3)
-            l_step(2)
-
-        @pl.when(tick == 7)
-        def _():
-            v_step(4)
-
-        @pl.when(tick == 8)
-        def _():
-            l_step(3)
-
-        @pl.when(tick == 9)
-        def _():
-            l_step(4)
-            join()
+    def sent():
+        for k in range(4):
+            w_ring(k, z, 0).wait_send()
+            if k < 3:
+                w_ring(k, z, 1).wait_send()
+            w_side(k, 0).wait_send()
+            w_side(k, 1).wait_send()
+            w_on(k).wait_send()
+        for n in range(CHUNKS):
+            w_twin(n, c).wait_send()
+        for d in range(3):
+            for cp in (g_y(d, y), g_mate(d, low, c), v_x(d, x), l_x(d, x), l_y(d, y)):
+                cp.wait_send()
+        for k in range(4):
+            v_ring(k, z, 0).wait_send()
+            if k < 3:
+                v_ring(k, z, 1).wait_send()
+        for k in range(3):
+            l_ring(k, z, 0).wait_send()
+            l_ring(k, z, 1).wait_send()
+        l_last(z, 0).wait_send()
+        l_last(z, 1).wait_send()
+        for zz in range(NZ):
+            v_twin(zz, c).wait_send()
+            l_twin(zz, c).wait_send()
+
+    def at_tick(tick, steps):
+        for when, do in steps.items():
+
+            @pl.when(tick == when)
+            def _(do=do):
+                for f, *k in do:
+                    f(*k)
 
     def toward(n):
         return lax.rem(y + 1 + 2 * lax.rem(n, 2), NY)
@@ -369,6 +332,8 @@
         q = 4 * xs + pair
         share(1, n).wait_recv()
         share(2, n).wait_recv()
+        for kind in range(3):
+            share(kind, n).wait_send()
         rem[q] = rem[q] - (decode(gi[n]) + decode(gd[n]))
 
     def each(tick, do):
@@ -379,8 +344,12 @@
         def _():
             do(n + 1)
 
+    load_w.wait()
     w_ring(0, z, 0).start()
     w_ring(0, z, 1).start()
+    load_dg.wait()
+    lx[x] = dg[...]
+    gb[low, c, y] = dg[:, pl.ds(pl.multiple_of(lax.div(t, 4) * 128, 128), 128)]
     for d in range(3):
         g_y(d, y).start()
     for d in range(3):
@@ -392,9 +361,9 @@
         g_mate(i, low, c).start()
     for d in range(3):
         l_x(d, lax.rem(x + 3 - d, NX)).wait_recv()
-    for xb in range(NX):
-        for d in range(3):
-            l_y(d, xb, y).start()
+    l_pack()
+    for d in range(3):
+        l_y(d, y).start()
     load_e.wait()
     load_x.wait()
 
@@ -412,7 +381,16 @@
             hand_out(n, 0)
             hand_out(n + 1, 1)
 
-        fetch(tick)
+        at_tick(tick, {
+            0: [(own_step, 1)],
+            1: [(own_step, 2)],
+            2: [(near_step, 1), (own_step, 3)],
+            4: [(l_step, 1), (near_step, 2)],
+            5: [(near_step, 3)],
+            7: [(far_step, 3), (v_step, 2)],
+            8: [(v_step, 3)],
+            9: [(l_step, 4)],
+        })
 
         @pl.when(jnp.logical_and(tick >= 1, tick <= TICKS))
         def _():
@@ -422,7 +400,17 @@
         def _():
             each(tick - 2, finish)
 
-        factor(tick)
+        at_tick(tick, {
+            0: [(invert,), (near_step, 0)],
+            1: [(l_step, 0)],
+            2: [(v_step, 0)],
+            4: [(v_step, 1), (far_step, 0), (far_step, 1)],
+            5: [(l_step, 2)],
+            6: [(far_step, 2)],
+            7: [(l_step, 3)],
+            8: [(v_step, 4)],
+            9: [(sent,), (join,)],
+        })
 
     def store(j):
         return pltpu.make_async_copy(ov.at[j], out_hbm.at[:, pl.ds(256 * j, 256)], out_s.at[j])
@@ -437,39 +425,11 @@
         store(j).start()
         oh, ol = split(o)
         for i in range(j + 1, 8):
-            block = lb[i // 2, pl.ds(4 * (i % 2), 4), :, :, :, pl.ds(256 * j, 256)].reshape(256, 256)
+            at_z, first = pl.ds(4 * (i % 2), 4), FIRST[i // 2] + 2 * j
+            block = jnp.concatenate([lp[at_z, :, first + b].reshape(256, 128) for b in (0, 1)], axis=1)
             u = dot_t(oh, block) + dot_t(ol, block)
             acc[i] = u if j == 0 else acc[i] + u
 
-    for k in range(4):
-        w_ring(k, z, 0).wait_send()
-        if k < 3:
-            w_ring(k, z, 1).wait_send()
-        w_side(k, 0).wait_send()
-        w_side(k, 1).wait_send()
-        w_on(k).wait_send()
-    for n in range(CHUNKS):
-        w_twin(n, c).wait_send()
-        for kind in range(3):
-            share(kind, n).wait_send()
-    for d in range(3):
-        for cp in (g_y(d, y), g_mate(d, low, c), v_x(d, x), l_x(d, x)):
-            cp.wait_send()
-        for xb in range(NX):
-            l_y(d, xb, y).wait_send()
-    for k in range(4):
-        v_ring(k, z, 0).wait_send()
-        if k < 3:
-            v_ring(k, z, 1).wait_send()
-        for xb in range(NX):
-            if k < 3 or xb in UPPER:
-                l_ring(k, xb, z, 0).wait_send()
-            if k < 3 or xb in LOWER:
-                l_ring(k, xb, z, 1).wait_send()
-    for zz in range(NZ):
-        v_twin(zz, c).wait_send()
-        for xb in range(NX):
-            l_twin(xb, zz, c).wait_send()
     for j in range(8):
         store(j).wait()
 
@@ -480,12 +440,14 @@
     scratch = [
         V((4 * TOK, COLS), bf16),
         V((TOK, WIN), bf16),
+        V((8, WIN), bf16),
         V((8, TOK, 256), f32),
         V((NX, NZ, 2, ROWS, COLS), bf16),
         V((2, 2, NY, 8, 128), bf16),
         V((2, 128, 128), bf16),
         V((NX, NZ, 2, 2, ROWS, 128), bf16),
-        V((NX, NZ, 2, NY, 8, WIN), bf16),
+        V((NX, 8, WIN), bf16),
+        V((NZ, 2, PACKED, NY, 8, 128), bf16),
         msg, msg, msg, msg, msg, msg,
         V((4 * TOK, 2 * CW), f32),
         V((4, TOK, CW), f32),
@@ -493,16 +455,16 @@
         V((8, 256, 256), bf16),
         V((8, 256, 256), bf16),
         V((8, TOK, 256), f32),
-        D((2,)), D((8,)),
+        D((4,)), D((8,)),
         D((2, 4)), D((8,)), D((2, 4)), D((3, 4)), D((4,)), D((CHUNKS,)), D((CHUNKS,)),
         D((3,)), D((3,)), D((3,)), D((3,)), D((3,)), D((3,)), D((2, 4)), D((8,)), D((8,)), D((8,)),
-        D((3,)), D((3,)), D((3, 4)), D((3, 4)), D((2, 4, 4)), D((8, 4)), D((8, 4)), D((8, 4)),
+        D((3,)), D((3,)), D((3,)), D((3,)), D((2, 4)), D((8, 2)), D((8,)), D((8,)),
         D((3, CHUNKS)), D((3, CHUNKS)),
     ]
     return pl.pallas_call(
         kernel,
         out_shape=jax.ShapeDtypeStruct((TOK, WIN), f32),
-        in_specs=[pl.BlockSpec(memory_space=pl.ANY)] * 2 + [pl.BlockSpec(memory_space=V)] * 2,
+        in_specs=[pl.BlockSpec(memory_space=pl.ANY)] * 4,
         out_specs=pl.BlockSpec(memory_space=pl.ANY),
         scratch_shapes=scratch,
         name="whiten",

time: 77.3 us -> 69.5 us (0.90)
  Pallas kernels: 74 us -> 66.2 us
    pallas_call x1, Pallas kernels: 74 us -> 66.2 us  [local(): pl.pallas_call(kernel, out_shape=jax.ShapeDtypeStruct((TOK, WIN), f32), i...]
where the time goes in v3:
time: 69.5 us; the launch traced here: 69.3 us
  Pallas kernels  66.2 us (95%)
  local copies, waits for them, and re-layouts  3.14 us (5%)
    pallas_call x1, Pallas kernels, local(): pl.pallas_call(kernel, out_shape=jax.ShapeDtypeStruct((TOK, WIN), f32), i...  66.2 us
    unnamed x1, local copies, waits for them, and re-layouts  3.14 us

profile of v3, /device:TPU:1, one launch (start us, length us, event | category | flops | bytes accessed | tf_op | source)
XLA Modules:
  0.0 69.3 jit_solution(8943750216310194202)
XLA Ops:
  0.0 66.2 %whiten.1 = f32[256,2048]{1,0:T(8,128)} custom-call(bf16[1024,1536]{1,0:T(8,128)(2,1)} %e_hbm.1, bf16[256,2048]{1,0:T(8,128)(2,1)} %x_hbm.1, bf16[32,1536]{1,0:T(8,128)(2,1)} %w_hbm.1, bf16[8,2048]{1,0:T(8,128)(2,1)} %dg_hbm.1), custom_call_target="tpu_custom_call" | custom-call | tf_op jit(solution)/shard_map/whiten/pallas_call | solution.py:464
  66.2 3.1 %copy.6 = f32[256,2048]{1,0:T(8,128)} copy(f32[256,2048]{1,0:T(8,128)} %whiten.1) | data formatting | bytes 4194304

commit v4 on v3

--- a/solution.py
+++ b/solution.py
@@ -9,7 +9,7 @@
 NX, NY, NZ = 4, 4, 8
 WIN, COLS, ROWS, TOK = 2048, 1536, 32, 256
 CHUNKS, CW = 16, 128
-TICKS = 9
+TICKS, LAG = 9, 2
 FLOOR = 2.0**-10
 
 
@@ -243,15 +243,19 @@
                 l_last(zsrc, way).start()
             l_twin(zsrc, c).start()
 
-    def join():
-        for zz in range(NZ):
-            v_twin(zz, 1 - c).wait_recv()
-            l_twin(zz, 1 - c).wait_recv()
-        for j in range(8):
-            xb, first = j // 2, 4 * (j % 2)
-            ah, al = (vb[xb, pl.ds(first, 2), :, h].reshape(128, 128) for h in (0, 1))
-            dh, dl = (vb[xb, pl.ds(first + 2, 2), :, h].reshape(128, 128) for h in (0, 1))
-            below = lp[pl.ds(first + 2, 2), :, FIRST[xb] + 2 * j].reshape(128, 128)
+    half = lax.div(z, 4)
+
+    def join(far):
+        side = 1 - half if far else half
+        for i in range(4):
+            v_twin(4 * side + i, 1 - c).wait_recv()
+            l_twin(4 * side + i, 1 - c).wait_recv()
+        for xb in range(NX):
+            j = 2 * xb + side
+            a, d = pl.ds(4 * side, 2), pl.ds(4 * side + 2, 2)
+            ah, al = (vb[xb, a, :, h].reshape(128, 128) for h in (0, 1))
+            dh, dl = (vb[xb, d, :, h].reshape(128, 128) for h in (0, 1))
+            below = lp[d, :, FIRST[xb] + 2 * j].reshape(128, 128)
             th, tl = split(dot(dh, below) + dot(dl, below))
             bh, bl = split(-(dot(th, ah) + (dot(th, al) + dot(tl, ah))))
             zero = jnp.zeros((128, 128), bf16)
@@ -367,7 +371,7 @@
     load_e.wait()
     load_x.wait()
 
-    @pl.loop(0, TICKS + 2)
+    @pl.loop(0, TICKS + LAG)
     def _(tick):
         @pl.when(tick < 2)
         def _():
@@ -383,33 +387,32 @@
 
         at_tick(tick, {
             0: [(own_step, 1)],
-            1: [(own_step, 2)],
-            2: [(near_step, 1), (own_step, 3)],
-            4: [(l_step, 1), (near_step, 2)],
+            1: [(own_step, 2), (l_step, 0)],
+            2: [(near_step, 1)],
+            4: [(l_step, 1), (far_step, 0), (near_step, 2), (v_step, 1)],
             5: [(near_step, 3)],
-            7: [(far_step, 3), (v_step, 2)],
+            6: [(far_step, 2)],
+            7: [(l_step, 3)],
             8: [(v_step, 3)],
-            9: [(l_step, 4)],
+            9: [(v_step, 4)],
         })
 
         @pl.when(jnp.logical_and(tick >= 1, tick <= TICKS))
         def _():
             each(tick - 1, pass_on)
 
-        @pl.when(tick >= 2)
+        @pl.when(tick >= LAG)
         def _():
-            each(tick - 2, finish)
+            each(tick - LAG, finish)
 
         at_tick(tick, {
             0: [(invert,), (near_step, 0)],
-            1: [(l_step, 0)],
-            2: [(v_step, 0)],
-            4: [(v_step, 1), (far_step, 0), (far_step, 1)],
+            2: [(v_step, 0), (own_step, 3)],
+            4: [(far_step, 1)],
             5: [(l_step, 2)],
-            6: [(far_step, 2)],
-            7: [(l_step, 3)],
-            8: [(v_step, 4)],
-            9: [(sent,), (join,)],
+            6: [(far_step, 3), (v_step, 2)],
+            8: [(l_step, 4), (join, False)],
+            9: [(join, True), (sent,)],
         })
 
     def store(j):

time: 69.5 us -> 68.2 us (0.981)
  Pallas kernels: 66.2 us -> 64.8 us
    pallas_call x1, Pallas kernels: 66.2 us -> 64.8 us  [local(): pl.pallas_call(kernel, out_shape=jax.ShapeDtypeStruct((TOK, WIN), f32), i...]
where the time goes in v4:
time: 68.2 us; the launch traced here: 68 us
  Pallas kernels  64.8 us (95%)
  local copies, waits for them, and re-layouts  3.14 us (5%)
    pallas_call x1, Pallas kernels, local(): pl.pallas_call(kernel, out_shape=jax.ShapeDtypeStruct((TOK, WIN), f32), i...  64.8 us
    unnamed x1, local copies, waits for them, and re-layouts  3.14 us

profile of v4, /device:TPU:1, one launch (start us, length us, event | category | flops | bytes accessed | tf_op | source)
XLA Modules:
  0.0 68.0 jit_solution(253415528413398588)
XLA Ops:
  0.0 64.8 %whiten.1 = f32[256,2048]{1,0:T(8,128)} custom-call(bf16[1024,1536]{1,0:T(8,128)(2,1)} %e_hbm.1, bf16[256,2048]{1,0:T(8,128)(2,1)} %x_hbm.1, bf16[32,1536]{1,0:T(8,128)(2,1)} %w_hbm.1, bf16[8,2048]{1,0:T(8,128)(2,1)} %dg_hbm.1), custom_call_target="tpu_custom_call" | custom-call | tf_op jit(solution)/shard_map/whiten/pallas_call | solution.py:467
  64.8 3.1 %copy.6 = f32[256,2048]{1,0:T(8,128)} copy(f32[256,2048]{1,0:T(8,128)} %whiten.1) | data formatting | bytes 4194304

commit v5 on v4

--- a/solution.py
+++ b/solution.py
@@ -412,7 +412,7 @@
             5: [(l_step, 2)],
             6: [(far_step, 3), (v_step, 2)],
             8: [(l_step, 4), (join, False)],
-            9: [(join, True), (sent,)],
+            9: [(join, True)],
         })
 
     def store(j):
@@ -433,6 +433,7 @@
             u = dot_t(oh, block) + dot_t(ol, block)
             acc[i] = u if j == 0 else acc[i] + u
 
+    sent()
     for j in range(8):
         store(j).wait()
 

time: 68.2 us -> 68.2 us (level)
  no operation moved by 1% of the time
where the time goes in v5:
time: 68.2 us; the launch traced here: 67.8 us
  Pallas kernels  64.7 us (95%)
  local copies, waits for them, and re-layouts  3.14 us (5%)
    pallas_call x1, Pallas kernels, local(): pl.pallas_call(kernel, out_shape=jax.ShapeDtypeStruct((TOK, WIN), f32), i...  64.7 us
    unnamed x1, local copies, waits for them, and re-layouts  3.14 us

profile of v5, /device:TPU:1, one launch (start us, length us, event | category | flops | bytes accessed | tf_op | source)
XLA Modules:
  0.0 67.8 jit_solution(14477615552978346926)
XLA Ops:
  0.0 64.7 %whiten.1 = f32[256,2048]{1,0:T(8,128)} custom-call(bf16[1024,1536]{1,0:T(8,128)(2,1)} %e_hbm.1, bf16[256,2048]{1,0:T(8,128)(2,1)} %x_hbm.1, bf16[32,1536]{1,0:T(8,128)(2,1)} %w_hbm.1, bf16[8,2048]{1,0:T(8,128)(2,1)} %dg_hbm.1), custom_call_target="tpu_custom_call" | custom-call | tf_op jit(solution)/shard_map/whiten/pallas_call | solution.py:468
  64.7 3.1 %copy.6 = f32[256,2048]{1,0:T(8,128)} copy(f32[256,2048]{1,0:T(8,128)} %whiten.1) | data formatting | bytes 4194304

commit v6 on v5

--- a/solution.py
+++ b/solution.py
@@ -9,7 +9,7 @@
 NX, NY, NZ = 4, 4, 8
 WIN, COLS, ROWS, TOK = 2048, 1536, 32, 256
 CHUNKS, CW = 16, 128
-TICKS, LAG = 9, 2
+TICKS, LAG = 9, 3
 FLOOR = 2.0**-10
 
 

time: 68.2 us -> 68.5 us (level)
  no operation moved by 1% of the time
where the time goes in v6:
time: 68.5 us; the launch traced here: 68.4 us
  Pallas kernels  65.2 us (95%)
  local copies, waits for them, and re-layouts  3.14 us (5%)
    pallas_call x1, Pallas kernels, local(): pl.pallas_call(kernel, out_shape=jax.ShapeDtypeStruct((TOK, WIN), f32), i...  65.2 us
    unnamed x1, local copies, waits for them, and re-layouts  3.14 us

profile of v6, /device:TPU:1, one launch (start us, length us, event | category | flops | bytes accessed | tf_op | source)
XLA Modules:
  0.0 68.4 jit_solution(5252443801570396044)
XLA Ops:
  0.0 65.2 %whiten.1 = f32[256,2048]{1,0:T(8,128)} custom-call(bf16[1024,1536]{1,0:T(8,128)(2,1)} %e_hbm.1, bf16[256,2048]{1,0:T(8,128)(2,1)} %x_hbm.1, bf16[32,1536]{1,0:T(8,128)(2,1)} %w_hbm.1, bf16[8,2048]{1,0:T(8,128)(2,1)} %dg_hbm.1), custom_call_target="tpu_custom_call" | custom-call | tf_op jit(solution)/shard_map/whiten/pallas_call | solution.py:468
  65.2 3.1 %copy.6 = f32[256,2048]{1,0:T(8,128)} copy(f32[256,2048]{1,0:T(8,128)} %whiten.1) | data formatting | bytes 4194304
